TPU v7x, 256 devices: a whole 4x4x8 slice. The times are simulated.
256 devices in a mesh: dp: 16 (over z, core), ctx: 16 (over y, x).
Axes of the slice: x: 4, y: 4, z: 8, core: 2. Of those that a mesh axis runs over, the one named last changes fastest.
Arguments:
- corpus: bfloat16 [4096, 3584], P('dp'), may hold values from -60 to 60
- owners: int32 [16, 2048, 1], P('dp', 'ctx'), may hold values from 0 to 15; in each aligned block of 128 rows (0 to 127, 128 to 255, ..., all dimensions but the last counted through in order) at most 16 rows name the same one
- local_rows: int32 [16, 2048], P('dp', 'ctx'), may hold values from 0 to 255
- doc_ids: int32 [16, 2048], P('dp'), may hold values from 0 to 15, never falling along the last dimension, each value on 1 to 512 neighbouring positions
- norm_gain: float32 [3584], replicated, may hold values from 0.1 to 1.9
- wqkv: bfloat16 [3584, 3072], P('dp'), may hold values from -3 to 3
- qkv_bias: float32 [3072], replicated, may hold values from -3 to 3
Outputs:
- context: bfloat16 [16, 2048, 2048], P('dp', 'ctx')
Inputs may be any that keep to these rules, and one draw needn't show every extreme that they name: `owners`: among the 128 positions of one device, at most 16 name one owner, a bound that some block reaches. `doc_ids`: document numbers never fall along a window; a document holds at most 512 positions, and one holds exactly that many.
All inputs are finite; a program needn't handle non-finite values.
Results may differ from a plain program's by a relative error of at most 0.0045.
The roundings to bfloat16 on the way count: a program that leaves them out, or rounds other values in their place, can miss the bound.
Values may be sent and summed in bfloat16 or wider, within the bound.
A program may use at most 128 MiB of HBM per device.

v0:
```python
import jax
import jax.numpy as jnp
from jax import lax
from jax.sharding import PartitionSpec as P

KEY_VALUE_HEADS = 4
HEAD_SIZE = 128
QUERY_HEADS = 16


EPS = 1e-06
ROPE_BASE = 1000000.0


def apply_rotary(tensor, token_positions):
    half_width = tensor.shape[-1] // 2
    frequency = ROPE_BASE ** (-jnp.arange(half_width, dtype=jnp.float32) * 2.0 / tensor.shape[-1])
    angles = token_positions.astype(jnp.float32)[:, None] * frequency[None, :]
    cosine = jnp.cos(angles)[:, None, :]
    sine_table = jnp.sin(angles)[:, None, :]
    leading = tensor[..., :half_width]
    trailing = tensor[..., half_width:]
    return jnp.concatenate(
        [leading * cosine - trailing * sine_table, trailing * cosine + leading * sine_table],
        axis=-1,
    )


def tile_scores(query_rows, key_part, query_pos, key_pos, query_lab, key_lab, score_scale):
    scores = (
        jnp.einsum("qnd,knd->nqk", query_rows, key_part, preferred_element_type=jnp.float32)
        * score_scale
    )
    visible = (query_lab[:, None] == key_lab[None, :]) & (key_pos[None, :] <= query_pos[:, None])
    return jnp.where(visible[None], scores, -jnp.inf)


def finish(mixture, running):
    return (mixture / jnp.transpose(running)[:, :, None]).astype(jnp.bfloat16)


def attend(items, labels):
    token_length = items.shape[0]
    head_count = items.shape[1]
    head_width = items.shape[2] // 3
    query_all = items[:, :, :head_width]
    key_all = items[:, :, head_width : 2 * head_width]
    value_all = items[:, :, 2 * head_width :]
    block_len = min(512, token_length)
    score_scale = head_width ** (-0.5)
    token_positions = jnp.arange(token_length, dtype=jnp.int32)

    def one_block(number):
        offset = number * block_len
        query_rows = lax.dynamic_slice_in_dim(query_all, offset, block_len, 0)
        query_pos = offset + jnp.arange(block_len, dtype=jnp.int32)
        query_lab = lax.dynamic_slice_in_dim(labels, offset, block_len, 0)
        scores = tile_scores(
            query_rows, key_all, query_pos, token_positions, query_lab, labels, score_scale
        )
        highest = jnp.max(scores, axis=2, keepdims=True)
        exponent = jnp.exp(scores - highest)
        weights = exponent.astype(jnp.bfloat16)
        mixture = jnp.einsum("nqk,knd->qnd", weights, value_all, preferred_element_type=jnp.float32)
        result = finish(mixture, jnp.sum(exponent, axis=2))
        return result

    blocks = lax.map(one_block, jnp.arange(token_length // block_len, dtype=jnp.int32))
    return blocks.reshape(token_length, head_count, head_width)


def per_device(corpus, owners, local_rows, doc_ids, norm_gain, wqkv, qkv_bias):
    dp_count = lax.axis_size("dp")
    ctx_count = lax.axis_size("ctx")
    owner_col = owners[0, :, 0]
    row_local = local_rows[0]
    token_count = row_local.shape[0]
    capacity = max(2, 2 * token_count // dp_count)
    choose = (owner_col[:, None] == jnp.arange(dp_count, dtype=jnp.int32)[None, :]).astype(
        jnp.int32
    )
    slot_num = jnp.sum((jnp.cumsum(choose, axis=0) - choose) * choose, axis=1)
    requests = jnp.zeros((dp_count, capacity), jnp.int32).at[owner_col, slot_num].set(row_local)
    asked_rows = lax.all_to_all(requests, "dp", split_axis=0, concat_axis=0, tiled=True)
    served = jnp.take(corpus, asked_rows.reshape(-1), axis=0).reshape(
        dp_count, capacity, corpus.shape[1]
    )
    returned = lax.all_to_all(served, "dp", split_axis=0, concat_axis=0, tiled=True)
    fetched = returned[owner_col, slot_num]
    floats = fetched.astype(jnp.float32)
    mean_square = jnp.mean(floats * floats, axis=-1, keepdims=True)
    normed = (floats * lax.rsqrt(mean_square + EPS) * norm_gain).astype(jnp.bfloat16)
    labels = doc_ids[0]
    group_width = QUERY_HEADS // KEY_VALUE_HEADS
    heads_here = QUERY_HEADS // ctx_count
    projected_input = (
        jnp.dot(
            normed,
            lax.all_gather(wqkv, "dp", axis=0, tiled=True),
            preferred_element_type=jnp.float32,
        )
        + qkv_bias
    )
    token_positions = lax.axis_index("ctx") * token_count + jnp.arange(token_count, dtype=jnp.int32)
    queries = apply_rotary(
        projected_input[:, : QUERY_HEADS * HEAD_SIZE].reshape(token_count, QUERY_HEADS, HEAD_SIZE),
        token_positions,
    ).astype(jnp.bfloat16)
    key_matrix = apply_rotary(
        projected_input[
            :, QUERY_HEADS * HEAD_SIZE : (QUERY_HEADS + KEY_VALUE_HEADS) * HEAD_SIZE
        ].reshape(token_count, KEY_VALUE_HEADS, HEAD_SIZE),
        token_positions,
    ).astype(jnp.bfloat16)
    value_matrix = (
        projected_input[:, (QUERY_HEADS + KEY_VALUE_HEADS) * HEAD_SIZE :]
        .reshape(token_count, KEY_VALUE_HEADS, HEAD_SIZE)
        .astype(jnp.bfloat16)
    )
    packed = jnp.concatenate(
        [
            queries,
            jnp.repeat(key_matrix, group_width, axis=1),
            jnp.repeat(value_matrix, group_width, axis=1),
        ],
        axis=2,
    )
    grouped = packed.reshape(token_count, ctx_count, heads_here, packed.shape[2])
    received = lax.all_to_all(grouped, "ctx", split_axis=1, concat_axis=0, tiled=True)
    flat = received.reshape(received.shape[0], received.shape[2], received.shape[3])
    attended = attend(flat, labels)
    context = lax.all_to_all(attended, "ctx", split_axis=0, concat_axis=1, tiled=True)
    return context.reshape(1, token_count, QUERY_HEADS * HEAD_SIZE)


def solution(mesh):
    return jax.shard_map(
        per_device,
        mesh=mesh,
        in_specs=(
            P("dp", None),
            P("dp", "ctx", None),
            P("dp", "ctx"),
            P("dp", None),
            P(),
            P("dp", None),
            P(),
        ),
        out_specs=P("dp", "ctx", None),
        check_vma=False,
    )
```

profile of v0, /device:TPU:1, one launch (start us, length us, event | category | flops | bytes accessed | tf_op | source)
XLA Modules:
  0.0 266.1 jit_solution(5231523373532456831)
XLA Ops:
  6.5 0.7 all-gather.2.cloned.1.call-update
  7.3 0.7 fusion.35
  8.0 0.2 reduce_window_sum.11
  8.2 0.8 select_reduce_fusion
  9.0 0.7 fusion.37
  9.7 11.1 %scatter_fusion = s32[16,16]{1,0:T(8,128)S(1)} fusion(s32[16,16]{1,0:T(8,128)S(1)} %broadcast_in_dim.25, s32[128]{0:T(128)S(1)} %get-tuple-element.87, s32[128]{0:T(128)} %bitcast.114), kind=kCustom, calls=%fused_computation.2 | custom fusion | bytes 2560 | tf_op jit(solution)/shard_map/scatter | solution.py:83
  20.8 16.9 %all_to_all.44 = s32[16,1,16]{2,1,0:T(1,128)S(1)} all-to-all(s32[16,1,16]{2,1,0:T(1,128)S(1)} %bitcast.96), channel_id=1, replica_groups=mesh['dp'=16,'ctx'=16] {'dp'}, dimensions={0} | all-to-all | bytes 2048 | tf_op jit(solution)/shard_map/all_to_all | solution.py:84
  37.7 0.5 broadcast.218
  38.2 0.7 reduce.7
  38.9 0.1 reshape.225
  39.0 3.0 %gather_fusion = bf16[256,3584]{1,0:T(8,128)(2,1)} fusion(bf16[256,3584]{1,0:T(8,128)(2,1)S(1)} %copy-done, s32[1024]{0:T(1024)S(1)} %pad_clamp_fusion), kind=kCustom, calls=%fused_computation | custom fusion | bytes 3671040 | tf_op jit(solution)/shard_map/jit(_take)/gather | solution.py:85
  42.0 3.0 %broadcast_select_fusion = bf16[16,16,3584]{2,1,0:T(8,128)(2,1)} fusion(bf16[16,16,3584]{2,1,0:T(8,128)(2,1)} %bitcast.99, pred[16,16]{1,0:T(8,128)(4,1)S(1)} %compare_and_fusion), kind=kLoop, calls=%fused_computation.29 | loop fusion | flops 917504 | bytes 3670272 | tf_op jit(solution)/shard_map/jit(_take)/select_n | solution.py:85
  45.0 4.8 %all-to-all-start.1 = ((bf16[16,16,3584]{2,1,0:T(8,128)(2,1)}), bf16[16,16,3584]{2,1,0:T(8,128)(2,1)}, u32[]{:S(2)}, u32[]{:S(2)}) async-start(bf16[16,16,3584]{2,1,0:T(8,128)(2,1)} %broadcast_select_fusion), calls=%async_computation.1 | async-start | bytes 3670016 | tf_op jit(solution)/shard_map/all_to_all | solution.py:88
  49.8 0.3 multiply_cosine_fusion
  50.1 61.9 %all-to-all-done.1 = bf16[16,16,3584]{2,1,0:T(8,128)(2,1)} async-done(((bf16[16,16,3584]{2,1,0:T(8,128)(2,1)}), bf16[16,16,3584]{2,1,0:T(8,128)(2,1)}, u32[]{:S(2)}, u32[]{:S(2)}) %all-to-all-start.1) | async-done | bytes 1835040 | tf_op jit(solution)/shard_map/all_to_all | solution.py:88
  112.0 3.5 %gather_fusion.1 = bf16[128,3584]{1,0:T(8,128)(2,1)S(1)} fusion(bf16[16,16,3584]{2,1,0:T(8,128)(2,1)} %all-to-all-done.1, s32[128]{0:T(128)S(1)} %bitcast.98), kind=kCustom, calls=%fused_computation.1 | custom fusion | bytes 1836032 | tf_op jit(solution)/shard_map/gather | solution.py:89
  115.5 0.3 fusion.28
  115.8 57.2 %all-gather.2.cloned.1.call-done = bf16[3584,3072]{1,0:T(8,128)(2,1)} async-done(((bf16[224,3072]{1,0:T(8,128)(2,1)}), bf16[3584,3072]{1,0:T(8,128)(2,1)}) %all-gather.2.cloned.1.call-update) | async-done | bytes 22020112 | tf_op jit(solution)/shard_map/all_gather | solution.py:99
  173.1 9.0 %convolution_add_fusion = f32[128,3072]{1,0:T(8,128)S(1)} fusion(bf16[3584,3072]{1,0:T(8,128)(2,1)} %all-gather.2.cloned.1.call-done, bf16[128,3584]{1,0:T(8,128)(2,1)S(1)} %gather_fusion.1, f32[3584]{0:T(1024)S(1)} %copy-done.4, f32[128]{0:T(128)S(1)} %add_rsqrt_fusion, f32[3072]{0:T(1024)S(1)} %copy-done.6), kind=kOutput, calls=%fused_computation.23 | convolution fusion | flops 2820800512 | bytes 24537600 | tf_op jit(solution)/shard_map/dot_general | solution.py:97
  182.1 0.1 slice_bitcast_fusion
  182.2 0.7 copy_bitcast_fusion
  182.8 0.1 reshape.227
  182.9 0.3 subtract_convert_fusion.1
  183.2 0.2 pad_maximum_fusion
  183.4 0.2 copy.41
  183.6 0.3 fusion.41
  184.0 0.7 subtract_convert_fusion
  184.7 0.1 broadcast_in_dim.28
  184.8 0.1 copy-done.2
  184.9 0.1 broadcast_in_dim.29
  185.0 1.7 maximum_bitcast_fusion
  186.7 6.5 %all-to-all-start.2 = ((bf16[128,16,1,384]{3,0,2,1:T(8,128)(2,1)}), bf16[128,16,1,384]{3,0,2,1:T(8,128)(2,1)S(1)}, u32[]{:S(2)}, u32[]{:S(2)}) async-start(bf16[128,16,1,384]{3,0,2,1:T(8,128)(2,1)} %maximum_bitcast_fusion), calls=%async_computation.2 | async-start | bytes 3145728 | tf_op jit(solution)/shard_map/all_to_all | solution.py:129
  193.3 24.6 %all-to-all-done.2 = bf16[128,16,1,384]{3,0,2,1:T(8,128)(2,1)S(1)} async-done(((bf16[128,16,1,384]{3,0,2,1:T(8,128)(2,1)}), bf16[128,16,1,384]{3,0,2,1:T(8,128)(2,1)S(1)}, u32[]{:S(2)}, u32[]{:S(2)}) %all-to-all-start.2) | async-done | bytes 1572896 | tf_op jit(solution)/shard_map/all_to_all | solution.py:129
  217.9 1.2 copy-done.1
  219.0 2.3 fusion.40
  221.4 20.2 %while.11 = (s32[]{:T(128)}, bf16[4,512,1,128]{3,1,2,0:T(8,128)(2,1)S(1)}, s32[4]{0:T(128)S(1)}, s32[2048]{0:T(1024)S(1)}, s32[1,2048]{1,0:T(1,128)S(1)}, /*inde...) while((s32[]{:T(128)}, ...), condition=%wide.region_7.8_spmd.clone, body=%wide.region_4.7_spmd.clone.sunk | while | flops 547487232 | bytes 13922495 | solution.py:68
  221.4 0.6 dynamic_slice.23
  222.6 0.1 dynamic_slice.24
  222.7 2.2 fusion.51
  224.8 0.7 fusion.52
  225.6 0.8 fusion.53
  226.4 0.6 dynamic_slice.23
  227.7 0.1 dynamic_slice.24
  227.8 2.2 fusion.51
  229.9 0.7 fusion.52
  230.6 0.8 fusion.53
  231.5 0.6 dynamic_slice.23
  232.7 0.1 dynamic_slice.24
  232.8 2.2 fusion.51
  235.0 0.7 fusion.52
  235.7 0.8 fusion.53
  236.5 0.6 dynamic_slice.23
  237.8 0.1 dynamic_slice.24
  237.9 2.2 fusion.51
  240.0 0.7 fusion.52
  240.7 0.8 fusion.53
  241.6 0.5 broadcast.223
  242.1 1.0 reduce.8
  243.1 0.1 reshape.266
  243.3 14.0 %all_to_all.45 = bf16[16,2,8192]{2,1,0:T(2,128)(2,1)S(1)} all-to-all(bf16[16,2,8192]{2,1,0:T(2,128)(2,1)S(1)} %reshape.266), channel_id=1, replica_groups=mesh['dp'=16,'ctx'=16] {'ctx'}, dimensions={0} | all-to-all | bytes 1048576 | tf_op jit(solution)/shard_map/all_to_all | solution.py:132
  257.3 0.5 reshape.267
  257.8 0.1 copy.37
  257.9 0.3 copy.35
  258.2 1.0 copy.36
  (28 shorter events, 0.1 us)
Async XLA Ops:
  6.5 32.4 %copy-start = (bf16[256,3584]{1,0:T(8,128)(2,1)S(1)}, bf16[256,3584]{1,0:T(8,128)(2,1)}, u32[]{:S(2)}) copy-start(bf16[256,3584]{1,0:T(8,128)(2,1)} %param.9) | copy-start | bytes 5505028
  6.5 166.5 %all-gather.2.cloned.1.call-start = ((), (), s32[]{:S(2)}) async-start(), calls=%async_computation.4 | async-start | bytes 23396352 | tf_op jit(solution)/shard_map/all_gather | solution.py:99
  45.0 67.0 %all-to-all-start.1 = ((bf16[16,16,3584]{2,1,0:T(8,128)(2,1)}), bf16[16,16,3584]{2,1,0:T(8,128)(2,1)}, u32[]{:S(2)}, u32[]{:S(2)}) async-start(bf16[16,16,3584]{2,1,0:T(8,128)(2,1)} %broadcast_select_fusion), calls=%async_computation.1 | async-start | bytes 3670016 | tf_op jit(solution)/shard_map/all_to_all | solution.py:88
  112.0 61.0 %copy-start.4 = (f32[3584]{0:T(1024)S(1)}, f32[3584]{0:T(1024)}, u32[]{:S(2)}) copy-start(f32[3584]{0:T(1024)} %param.13) | copy-start | bytes 43012
  112.0 61.0 %copy-start.6 = (f32[3072]{0:T(1024)S(1)}, f32[3072]{0:T(1024)}, u32[]{:S(2)}) copy-start(f32[3072]{0:T(1024)} %param.15) | copy-start | bytes 36868
  184.0 0.9 copy-start.2
  186.7 31.1 %all-to-all-start.2 = ((bf16[128,16,1,384]{3,0,2,1:T(8,128)(2,1)}), bf16[128,16,1,384]{3,0,2,1:T(8,128)(2,1)S(1)}, u32[]{:S(2)}, u32[]{:S(2)}) async-start(bf16[128,16,1,384]{3,0,2,1:T(8,128)(2,1)} %maximum_bitcast_fusion), calls=%async_computation.2 | async-start | bytes 3145728 | tf_op jit(solution)/shard_map/all_to_all | solution.py:129
  193.3 28.1 %copy-start.5 = (s32[1,2048]{1,0:T(1,128)S(1)}, s32[1,2048]{1,0:T(1,128)}, u32[]{:S(2)}) copy-start(s32[1,2048]{1,0:T(1,128)} %param.12) | copy-start | bytes 24580
  217.9 1.2 copy-start.1
  219.0 2.3 copy-start.3
Sparse Core Ops, SparseCore 0:
  9.2 163.8 all-gather.1
where the time goes:
time: 267 us; the launch traced here: 266 us
  waiting for transfers between devices  144 us (54%)
  blocking collectives  30.9 us (12%)
  local copies, waits for them, and re-layouts  28.6 us (11%)
  matrix products  21 us (8%)
  between operations  13.6 us (5%)
  other arithmetic  13.5 us (5%)
  starting transfers between devices  11.3 us (4%)
  loops' own time  2.7 us (1%)
    all_to_all x1, waiting for transfers between devices, per_device(): lax.all_to_all(served, 'dp', split_axis=0, concat_axis=0, tiled=True)  61.9 us
    all_gather x1, waiting for transfers between devices, per_device(): lax.all_gather(wqkv, 'dp', axis=0, tiled=True)  57.2 us
    all_to_all x1, waiting for transfers between devices, per_device(): lax.all_to_all(grouped, 'ctx', split_axis=1, concat_axis=0, tiled=True)  24.6 us
    all_to_all x1, blocking collectives, per_device(): lax.all_to_all(requests, 'dp', split_axis=0, concat_axis=0, tiled=True)  16.9 us
    all_to_all x1, blocking collectives, per_device(): lax.all_to_all(attended, 'ctx', split_axis=0, concat_axis=1, tiled=True)  14 us
    scatter x1, local copies, waits for them, and re-layouts, per_device(): jnp.zeros((dp_count, capacity), jnp.int32).at[owner_col, slot_num]  11.1 us
    dot_general x1, matrix products, per_device(): jnp.dot(normed, lax.all_gather(wqkv, 'dp', axis=0, tiled=True), preferred...  8.97 us
    dot_general x4, matrix products, tile_scores(): jnp.einsum('qnd,knd->nqk', query_rows, key_part, preferred_element_type=j...  8.62 us
  transfers between devices with their start and end apart: 3, of which 3 were waited for; matrix products, arithmetic and copies ran while one was open for 9% of the time, Pallas kernels for 0%

commit v1 on v0

v1 whole, which is shorter than its diff:
```python
import functools

import jax
import jax.numpy as jnp
import numpy as np
from jax import lax
from jax.experimental import pallas as pl
from jax.experimental.pallas import tpu as pltpu
from jax.sharding import PartitionSpec as P

KEY_VALUE_HEADS = 4
HEAD_SIZE = 128
QUERY_HEADS = 16
GROUP = QUERY_HEADS // KEY_VALUE_HEADS
EPS = 1e-06
ROPE_BASE = 1000000.0
MESH = pl.DeviceIdType.MESH
BLOCK = 128
REACH = 512
LOG2E = 1.4426950408889634


def rotary_tables(length):
    half = HEAD_SIZE // 2
    frequency = (ROPE_BASE ** (-np.arange(half, dtype=np.float64) * 2.0 / HEAD_SIZE)).astype(np.float32)
    angles = (np.arange(length, dtype=np.float32)[:, None] * frequency[None, :]).astype(np.float64)
    cosine, sine = np.cos(angles), np.sin(angles)
    return (
        np.concatenate([cosine, cosine], axis=1).astype(np.float32),
        np.concatenate([-sine, sine], axis=1).astype(np.float32),
    )


def rotate(rows, cosine, sine):
    return rows * cosine + pltpu.roll(rows, HEAD_SIZE // 2, 1) * sine


def attend_kernel(
    n_ctx, index_ref, table_ref, labels_ref, cos_ref, sin_ref, out_ref,
    picked, query_buf, key_buf, value_buf, label_buf, block_buf, send_sem, recv_sem,
):
    dp = lax.axis_index("dp")
    me = lax.axis_index("ctx")
    length = index_ref.shape[0] * index_ref.shape[1]
    blocks = length // BLOCK
    pad = REACH

    barrier = pltpu.get_barrier_semaphore()

    def greet(step, carry):
        pl.semaphore_signal(barrier, inc=1, device_id=(dp, lax.rem(me + step, n_ctx)), device_id_type=MESH)
        return carry

    lax.fori_loop(1, n_ctx, greet, 0)

    unroll = 16

    def pick(block, carry):
        def some(part, inner):
            for u in range(unroll):
                row = part * unroll + u
                target = pl.multiple_of((block * BLOCK + row) * 4, 4)
                picked[pl.ds(target, 4), :] = table_ref[index_ref[block, row]]
            return inner

        return lax.fori_loop(0, BLOCK // unroll, some, carry)

    lax.fori_loop(0, blocks, pick, 0)

    key_buf[pl.ds(0, pad), :] = jnp.zeros((pad, HEAD_SIZE), jnp.bfloat16)
    value_buf[pl.ds(0, pad), :] = jnp.zeros((pad, HEAD_SIZE), jnp.bfloat16)
    label_buf[...] = jnp.full(label_buf.shape, -1, jnp.int32)
    for block in range(blocks):
        label_buf[pl.ds(pad // BLOCK + block, 1), 0, :] = labels_ref[:, pl.ds(block * BLOCK, BLOCK)]

    def turn(block, carry):
        start = pl.multiple_of(block * BLOCK, BLOCK)
        cosine = cos_ref[pl.ds(start, BLOCK), :]
        sine = sin_ref[pl.ds(start, BLOCK), :]
        base = pl.multiple_of(start * 4, BLOCK)
        query_buf[pl.ds(start, BLOCK), :] = rotate(
            picked[pl.ds(base, BLOCK, stride=4), :], cosine, sine
        ).astype(jnp.bfloat16)
        key_buf[pl.ds(pad + start, BLOCK), :] = rotate(
            picked[pl.ds(base + 1, BLOCK, stride=4), :], cosine, sine
        ).astype(jnp.bfloat16)
        value_buf[pl.ds(pad + start, BLOCK), :] = picked[pl.ds(base + 2, BLOCK, stride=4), :].astype(jnp.bfloat16)
        return carry

    lax.fori_loop(0, blocks, turn, 0)
    pl.semaphore_wait(barrier, n_ctx - 1)

    reach_blocks = pad // BLOCK
    causal = lax.broadcasted_iota(jnp.int32, (BLOCK, BLOCK), 1) <= lax.broadcasted_iota(
        jnp.int32, (BLOCK, BLOCK), 0
    )
    factor = HEAD_SIZE ** (-0.5) * LOG2E

    def one_block(block):
        start = pl.multiple_of(block * BLOCK, BLOCK)
        query = query_buf[pl.ds(start, BLOCK), :]
        keys = key_buf[pl.ds(start, pad + BLOCK), :]
        values = value_buf[pl.ds(start, pad + BLOCK), :]
        query_labels = jnp.transpose(
            jnp.broadcast_to(label_buf[block + reach_blocks], (BLOCK, BLOCK)).astype(jnp.float32)
        )
        scores = lax.dot_general(
            query, keys, (((1,), (1,)), ((), ())), preferred_element_type=jnp.float32
        )
        parts = []
        for number in range(reach_blocks + 1):
            part = scores[:, number * BLOCK : (number + 1) * BLOCK]
            key_labels = jnp.broadcast_to(label_buf[block + number], (BLOCK, BLOCK)).astype(jnp.float32)
            visible = key_labels == query_labels
            if number == reach_blocks:
                visible = visible & causal
            parts.append(jnp.where(visible, part, -jnp.inf))
        highest = functools.reduce(jnp.maximum, parts)
        highest = jnp.max(highest, axis=1, keepdims=True)
        exponents = [jnp.exp2((part - highest) * factor) for part in parts]
        total = jnp.sum(functools.reduce(jnp.add, exponents), axis=1, keepdims=True)
        weights = jnp.concatenate([e.astype(jnp.bfloat16) for e in exponents], axis=1)
        mixture = jnp.dot(weights, values, preferred_element_type=jnp.float32)
        return (mixture / total).astype(jnp.bfloat16)

    def block_copy(step):
        block = lax.rem(me + step, n_ctx)
        return pltpu.make_async_remote_copy(
            src_ref=block_buf.at[step],
            dst_ref=out_ref.at[:, pl.ds(pl.multiple_of(me * HEAD_SIZE, HEAD_SIZE), HEAD_SIZE)],
            send_sem=send_sem.at[step],
            recv_sem=recv_sem.at[step],
            device_id=(dp, block),
            device_id_type=MESH,
        )

    def work(step, carry):
        block_buf[step] = one_block(lax.rem(me + step, n_ctx))
        block_copy(step).start()
        return carry

    lax.fori_loop(1, n_ctx, work, 0)
    out_ref[:, pl.ds(pl.multiple_of(me * HEAD_SIZE, HEAD_SIZE), HEAD_SIZE)] = one_block(me)

    def finish(step, carry):
        block_copy(step).wait()
        return carry

    lax.fori_loop(1, n_ctx, finish, 0)


def attend(n_ctx, index, table, labels, cosine, sine):
    length = index.shape[0] * index.shape[1]
    vmem = pl.BlockSpec(memory_space=pltpu.VMEM)
    return pl.pallas_call(
        functools.partial(attend_kernel, n_ctx),
        out_shape=jax.ShapeDtypeStruct((length // n_ctx, QUERY_HEADS * HEAD_SIZE), jnp.bfloat16),
        in_specs=[pl.BlockSpec(memory_space=pltpu.SMEM), vmem, vmem, vmem, vmem],
        out_specs=vmem,
        scratch_shapes=[
            pltpu.VMEM((length * 4, HEAD_SIZE), jnp.float32),
            pltpu.VMEM((length, HEAD_SIZE), jnp.bfloat16),
            pltpu.VMEM((REACH + length, HEAD_SIZE), jnp.bfloat16),
            pltpu.VMEM((REACH + length, HEAD_SIZE), jnp.bfloat16),
            pltpu.VMEM(((REACH + length) // BLOCK, 1, BLOCK), jnp.int32),
            pltpu.VMEM((n_ctx, BLOCK, HEAD_SIZE), jnp.bfloat16),
            pltpu.SemaphoreType.DMA((n_ctx,)),
            pltpu.SemaphoreType.DMA((n_ctx,)),
        ],
        compiler_params=pltpu.CompilerParams(
            collective_id=0, has_side_effects=True, vmem_limit_bytes=48 * 1024 * 1024
        ),
    )(index, table, labels, cosine, sine)


def per_device(corpus, owners, local_rows, doc_ids, norm_gain, wqkv, qkv_bias):
    n_ctx = lax.axis_size("ctx")
    ctx = lax.axis_index("ctx")
    corpus_rows = corpus.shape[0]
    index = owners[0, :, 0] * corpus_rows + local_rows[0]
    index = lax.all_gather(index, "ctx", axis=0, tiled=False)
    floats = corpus.astype(jnp.float32)
    mean_square = jnp.mean(floats * floats, axis=-1, keepdims=True)
    normed = (floats * lax.rsqrt(mean_square + EPS) * norm_gain).astype(jnp.bfloat16)
    starts = [
        ctx * HEAD_SIZE,
        (QUERY_HEADS + ctx // GROUP) * HEAD_SIZE,
        (QUERY_HEADS + KEY_VALUE_HEADS + ctx // GROUP) * HEAD_SIZE,
    ]
    columns = jnp.concatenate([lax.dynamic_slice_in_dim(wqkv, s, HEAD_SIZE, 1) for s in starts], axis=1)
    bias = jnp.concatenate([lax.dynamic_slice_in_dim(qkv_bias, s, HEAD_SIZE, 0) for s in starts])
    columns = lax.all_gather(columns, "dp", axis=0, tiled=True)
    projected = jnp.dot(normed, columns, preferred_element_type=jnp.float32) + bias
    projected = lax.all_gather(projected, "dp", axis=0, tiled=True)
    table = jnp.pad(projected, ((0, 0), (0, HEAD_SIZE))).reshape(-1, 4, HEAD_SIZE)
    length = index.shape[0] * index.shape[1]
    cosine, sine = rotary_tables(length)
    return attend(n_ctx, index, table, doc_ids, jnp.asarray(cosine), jnp.asarray(sine))[None]


def solution(mesh):
    return jax.shard_map(
        per_device,
        mesh=mesh,
        in_specs=(
            P("dp", None),
            P("dp", "ctx", None),
            P("dp", "ctx"),
            P("dp", None),
            P(),
            P("dp", None),
            P(),
        ),
        out_specs=P("dp", "ctx", None),
        check_vma=False,
    )
```

time: 267 us -> 151 us (0.57)
  waiting for transfers between devices: 144 us -> 70.8 us
  Pallas kernels: 0 us -> 23.3 us
  matrix products: 21 us -> 3.69 us
  blocking collectives: 30.9 us -> 16.8 us
  starting transfers between devices: 11.3 us -> 0.04 us
  other arithmetic: 13.5 us -> 2.66 us
  local copies, waits for them, and re-layouts: 28.6 us -> 19.9 us
  loops' own time: 2.7 us -> 0 us
    all_to_all x2 -> x0, waiting for transfers between devices: 86.5 us -> none  [the longest x1 61.9 us: per_device(): lax.all_to_all(served, 'dp', split_axis=0, concat_axis=0, tiled=True)]
    all_to_all x2 -> x0, blocking collectives: 30.9 us -> none  [the longest x1 16.9 us: per_device(): lax.all_to_all(requests, 'dp', split_axis=0, concat_axis=0, tiled=True)]
    pallas_call x0 -> x1, Pallas kernels: none -> 23.3 us  [attend(): pl.pallas_call(functools.partial(attend_kernel, n_ctx), out_shape=jax.Sha...]
    dot_general x9 -> x1, matrix products: 21 us -> 3.69 us  [per_device(): jnp.dot(normed, columns, preferred_element_type=jnp.float32) + bias]
    all_gather x0 -> x1, blocking collectives: none -> 16.8 us  [per_device(): index = lax.all_gather(index, 'ctx', axis=0, tiled=False)]
    all_gather x1 -> x2, waiting for transfers between devices: 57.2 us -> 70.7 us  [the longest x1 42.8 us: per_device(): columns = lax.all_gather(columns, 'dp', axis=0, tiled=True)]
    all_to_all x2 -> x0, starting transfers between devices: 11.3 us -> none  [the longest x1 6.54 us: per_device(): lax.all_to_all(grouped, 'ctx', split_axis=1, concat_axis=0, tiled=True)]
    scatter x1 -> x0, local copies, waits for them, and re-layouts: 11.1 us -> none  [per_device(): jnp.zeros((dp_count, capacity), jnp.int32).at[owner_col, slot_num]]
  transfers between devices with their start and end apart: 3 -> 2, of which waited for: 3 -> 2; matrix products, arithmetic and copies ran while one was open for 9% -> 2% of each run, Pallas kernels for 0% -> 0%
where the time goes in v1:
time: 151 us
  waiting for transfers between devices  70.8 us (47%)
  Pallas kernels  23.3 us (15%)
  local copies, waits for them, and re-layouts  19.9 us (13%)
  blocking collectives  16.8 us (11%)
  between operations  13.5 us (9%)
  matrix products  3.69 us (2%)
  other arithmetic  2.66 us (2%)
    all_gather x1, waiting for transfers between devices, per_device(): columns = lax.all_gather(columns, 'dp', axis=0, tiled=True)  42.8 us
    all_gather x1, waiting for transfers between devices, per_device(): projected = lax.all_gather(projected, 'dp', axis=0, tiled=True)  28 us
    pallas_call x1, Pallas kernels, attend(): pl.pallas_call(functools.partial(attend_kernel, n_ctx), out_shape=jax.Sha...  23.3 us
    all_gather x1, blocking collectives, per_device(): index = lax.all_gather(index, 'ctx', axis=0, tiled=False)  16.8 us
    reshape x1, local copies, waits for them, and re-layouts, per_device(): jnp.pad(projected, ((0, 0), (0, HEAD_SIZE))).reshape(-1, 4, HEAD_SIZE)  10.1 us
    pad x1, local copies, waits for them, and re-layouts, per_device(): jnp.pad(projected, ((0, 0), (0, HEAD_SIZE))).reshape(-1, 4, HEAD_SIZE)  7.17 us
    dot_general x1, matrix products, per_device(): jnp.dot(normed, columns, preferred_element_type=jnp.float32) + bias  3.69 us
  transfers between devices with their start and end apart: 2, of which 2 were waited for; matrix products, arithmetic and copies ran while one was open for 2% of the time, Pallas kernels for 0%

profile of v1, /device:TPU:1, one launch (start us, length us, event | category | flops | bytes accessed | tf_op | source)
XLA Modules:
  0.0 150.6 jit_solution(6162659543099539652)
XLA Ops:
  6.5 0.0 copy-start.3
  6.5 0.0 copy-start.4
  6.5 0.0 all-gather.4.cloned.1.call-start
  6.5 1.0 constant_dynamic-slice_fusion.2
  7.6 0.7 pad_maximum_fusion
  8.3 0.0 all-gather.4.cloned.1.call-update
  8.3 0.0 all-gather.6.cloned.1.call-start
  8.3 0.8 fusion.11
  9.2 1.9 %fusion = f32[256]{0:T(256)S(1)} fusion(bf16[256,3584]{1,0:T(8,128)(2,1)} %param.9), kind=kLoop, calls=%fused_computation.2 | loop fusion | flops 2752256 | bytes 1836032 | tf_op jit(solution)/shard_map/reduce_sum | solution.py:183
  11.1 0.0 copy-start.5
  11.2 0.0 copy-start.6
  11.2 42.8 %all-gather.4.cloned.1.call-done = bf16[3584,384]{1,0:T(8,128)(2,1)} async-done(((bf16[224,384]{1,0:T(8,128)(2,1)}), bf16[3584,384]{1,0:T(8,128)(2,1)}) %all-gather.4.cloned.1.call-update) | async-done | bytes 2752528 | tf_op jit(solution)/shard_map/all_gather | solution.py:192
  53.9 0.0 copy-done.3
  53.9 0.0 copy-done.4
  53.9 3.7 %fusion.7 = f32[256,384]{1,0:T(8,128)} fusion(bf16[3584,384]{1,0:T(8,128)(2,1)} %all-gather.4.cloned.1.call-done, bf16[256,3584]{1,0:T(8,128)(2,1)S(1)} %copy-done.3, f32[3584]{0:T(1024)S(1)} %copy-done.4, f32[256]{0:T(256)S(1)} %add_rsqrt_fusion, f32[384]{0:T(512)S(1)} %pad_maximum_fusion.1), kind=kOutput, calls=%fused_computation.8 | convolution fusion | flops 708411392 | bytes 4997632 | tf_op jit(solution)/shard_map/dot_general | solution.py:193
  57.6 0.0 all-gather.6.cloned.1.call-update
  57.7 0.0 copy-done.5
  57.7 0.0 copy-done.6
  57.7 16.8 %all-gather = s32[16,1,128]{2,1,0:T(1,128)S(1)} all-gather(s32[1,1,128]{2,1,0:T(1,128)S(1)} %fusion.10), channel_id=1, replica_groups=mesh['dp'=16,'ctx'=16] {'ctx'}, dimensions={0}, use_global_device_ids=true | all-gather | bytes 8704 | tf_op jit(solution)/shard_map/all_gather | solution.py:181
  74.5 28.0 %all-gather.6.cloned.1.call-done = f32[4096,384]{1,0:T(8,128)} async-done(((f32[256,384]{1,0:T(8,128)}), f32[4096,384]{1,0:T(8,128)}) %all-gather.6.cloned.1.call-update) | async-done | bytes 6291472 | tf_op jit(solution)/shard_map/all_gather | solution.py:194
  102.4 7.2 %pad.4 = f32[4096,512]{1,0:T(8,128)} pad(f32[4096,384]{1,0:T(8,128)} %all-gather.6.cloned.1.call-done, f32[]{:T(128)} %constant.32.clone.1), padding=0_0x0_128 | pad | bytes 14680068 | tf_op jit(solution)/shard_map/jit(_pad)/pad | solution.py:195
  109.6 0.0 copy-start
  109.6 0.0 copy-start.1
  109.6 0.0 copy-start.2
  109.6 10.1 %reshape.25.table_ref = f32[4096,4,128]{2,1,0:T(4,128)} reshape(f32[4096,512]{1,0:T(8,128)} %pad.4) | data formatting | bytes 16777216 | tf_op jit(solution)/shard_map/reshape | solution.py:195
  119.7 0.0 copy-done
  119.7 0.0 copy-done.1
  119.7 0.0 copy-done.2
  119.7 23.3 %shard_map.91 = bf16[128,2048]{1,0:T(8,128)(2,1)S(1)} custom-call(s32[16,128]{1,0:T(8,128)S(1)} %bitcast.10, f32[4096,4,128]{2,1,0:T(4,128)} %reshape.25.table_ref, s32[1,2048]{1,0:T(1,128)S(1)} %copy-done.2, f32[2048,128]{1,0:T(8,128)S(1)} %copy-done, f32[2048,128]{1,0:T(8,128)S(1)} %copy-done.1), custom_call_target="tpu_custom_call" | custom-call | tf_op jit(solution)/shard_map/pallas_call | solution.py:155
  143.0 0.8 copy.12
  (3 shorter events, 0.0 us)
Async XLA Ops:
  6.5 47.4 %copy-start.3 = (bf16[256,3584]{1,0:T(8,128)(2,1)S(1)}, bf16[256,3584]{1,0:T(8,128)(2,1)}, u32[]{:S(2)}) copy-start(bf16[256,3584]{1,0:T(8,128)(2,1)} %param.9) | copy-start | bytes 5505028
  6.5 47.4 %copy-start.4 = (f32[3584]{0:T(1024)S(1)}, f32[3584]{0:T(1024)}, u32[]{:S(2)}) copy-start(f32[3584]{0:T(1024)} %param.13) | copy-start | bytes 43012
  6.5 47.4 %all-gather.4.cloned.1.call-start = ((), (), s32[]{:S(2)}) async-start(), calls=%async_computation | async-start | bytes 2924544 | tf_op jit(solution)/shard_map/all_gather | solution.py:192
  8.3 94.1 %all-gather.6.cloned.1.call-start = ((), (), s32[]{:S(2)}) async-start(), calls=%async_computation.1 | async-start | bytes 6684672 | tf_op jit(solution)/shard_map/all_gather | solution.py:194
  11.1 46.5 %copy-start.5 = (s32[1,128]{1,0:T(1,128)S(1)}, s32[1,128]{1,0:T(1,128)}, u32[]{:S(2)}) copy-start(s32[1,128]{1,0:T(1,128)} %param.11) | copy-start | bytes 1540
  11.2 46.5 %copy-start.6 = (s32[1,128,1]{1,2,0:T(1,128)S(1)}, s32[1,128,1]{1,2,0:T(1,128)}, u32[]{:S(2)}) copy-start(s32[1,128,1]{1,2,0:T(1,128)} %param.10) | copy-start | bytes 1540
  109.6 10.1 %copy-start = (f32[2048,128]{1,0:T(8,128)S(1)}, f32[2048,128]{1,0:T(8,128)}, u32[]{:S(2)}) copy-start(f32[2048,128]{1,0:T(8,128)} %constant.45.clone.cos_ref) | copy-start | bytes 3145732
  109.6 10.1 %copy-start.1 = (f32[2048,128]{1,0:T(8,128)S(1)}, f32[2048,128]{1,0:T(8,128)}, u32[]{:S(2)}) copy-start(f32[2048,128]{1,0:T(8,128)} %constant.46.clone.sin_ref) | copy-start | bytes 3145732
  109.6 10.1 %copy-start.2 = (s32[1,2048]{1,0:T(1,128)S(1)}, s32[1,2048]{1,0:T(1,128)}, u32[]{:S(2)}) copy-start(s32[1,2048]{1,0:T(1,128)} %labels_ref.1) | copy-start | bytes 24580
Sparse Core Ops, SparseCore 0:
  9.2 44.7 all-gather.3
  57.8 44.6 all-gather.5
